TPU v7x, 32 devices: a whole 2x2x4 slice. The times are simulated.
32 devices in a mesh: grp: 4 (over y, x), row: 8 (over z, core).
Axes of the slice: x: 2, y: 2, z: 4, core: 2. Of those that a mesh axis runs over, the one named last changes fastest.
Arguments:
- t_start: bfloat16 [8192, 512], P(('row', 'grp')), may hold values from -6 to 6
- h_blocks: bfloat16 [64, 4, 8, 128, 128], P('row', 'grp'), may hold values from -0.09375 to 0.09375
- h_cols: int32 [64, 4, 8], P('row', 'grp'), may hold values from 0 to 63, as said below
- t_cols: int32 [64, 3], P(('row', 'grp')), may hold values from 0 to 3, as said below
Outputs:
- t_before: bfloat16 [8192, 512], P(('row', 'grp'))
- t_last: bfloat16 [8192, 512], P(('row', 'grp'))
Inputs may be any that keep to these rules, and one draw needn't show every extreme that they name: The 8 entries of h_cols[b, g] differ, and each names a block row c with (c // 2) % 4 == g. `t_cols`: the 3 entries of a row differ.
All inputs are finite; a program needn't handle non-finite values.
Results may differ from a plain program's by a relative error of at most 0.025.
Values may be sent and summed in bfloat16 or wider, within the bound.
A program may use at most 64 MiB of HBM per device.

v0:
```python
import jax
import jax.numpy as jnp
from jax import lax
from jax.sharding import PartitionSpec as P

BS = 128
STEPS = 3


def per_device(t_start, h_blocks, h_cols, t_cols):
    groups = lax.axis_size("grp")
    rows_here = t_start.shape[0] // BS
    width = t_start.shape[1]
    col_blocks = width // BS
    blocks = h_blocks[:, 0]
    columns = h_cols[:, 0]
    local_index = columns // (groups * rows_here) * rows_here + columns % rows_here
    block_ids = jnp.arange(col_blocks, dtype=jnp.int32)
    kept = jnp.any(t_cols[:, :, None] == block_ids[None, None, :], axis=1)
    keep = kept.astype(jnp.float32)[:, None, :, None]

    def masked(values):
        shaped = values.reshape(rows_here, BS, col_blocks, BS) * keep
        return shaped.reshape(rows_here * BS, width)

    def apply_slab(slab):
        gathered = lax.all_gather(slab, "row", axis=0, tiled=True).reshape(-1, BS, width)
        picked = gathered[local_index]
        result = jnp.einsum("rsij,rsjm->rim", blocks, picked, preferred_element_type=jnp.float32)
        summed = lax.psum_scatter(
            result.astype(jnp.bfloat16).astype(jnp.float32).astype(jnp.bfloat16),
            "grp",
            scatter_dimension=0,
            tiled=True,
        ).astype(jnp.float32)
        return summed.reshape(rows_here * BS, width)

    first = masked(apply_slab(t_start)).astype(jnp.bfloat16)
    before, latest = (t_start, first)
    for step in range(STEPS - 1):
        summed = apply_slab(latest)
        after = masked(2.0 * summed - before.astype(jnp.float32)).astype(jnp.bfloat16)
        before, latest = (latest, after)
    return (before, latest)


def solution(mesh):
    placed = (
        P(("row", "grp"), None),
        P("row", "grp", None, None, None),
        P("row", "grp", None),
        P(("row", "grp"), None),
    )
    return jax.shard_map(
        per_device,
        mesh=mesh,
        in_specs=placed,
        out_specs=(P(("row", "grp"), None), P(("row", "grp"), None)),
        check_vma=False,
    )
```

profile of v0, /device:TPU:0, one launch (start us, length us, event | category | flops | bytes accessed | tf_op | source)
XLA Modules:
  0.0 241.7 jit_solution(15152453608066359497)
XLA Ops:
  7.2 0.0 all-gather.4.cloned.1.call-start
  7.2 0.7 all-gather.4.cloned.1.call-update
  7.9 0.0 reduce-scatter.4.cloned.1.call-start
  8.0 0.7 compare_select_fusion
  8.7 0.1 reshape.162
  8.8 32.7 %all-gather.4.cloned.1.call-done = bf16[2048,512]{1,0:T(8,128)(2,1)} async-done(((bf16[256,512]{1,0:T(8,128)(2,1)}), bf16[2048,512]{1,0:T(8,128)(2,1)}) %all-gather.4.cloned.1.call-update) | async-done | bytes 2097168 | tf_op jit(solution)/shard_map/all_gather | solution.py:27
  41.4 7.1 %gather_fusion = bf16[64,128,512]{2,1,0:T(8,128)(2,1)} fusion(bf16[16,128,512]{2,1,0:T(8,128)(2,1)} %bitcast.77, s32[1024]{0:T(1024)S(1)} %pad_clamp_fusion), kind=kCustom, calls=%fused_computation | custom fusion | bytes 16777472 | tf_op jit(solution)/shard_map/gather | solution.py:28
  48.6 7.1 %fusion.12 = bf16[8,128,512]{1,2,0:T(8,128)(2,1)} fusion(bf16[8,8,128,512]{3,2,1,0:T(8,128)(2,1)} %bitcast.81, bf16[8,1,8,128,128]{4,3,2,1,0:T(8,128)(2,1)S(1)} %copy-done), kind=kOutput, calls=%fused_computation.12 | convolution fusion | flops 1074266112 | bytes 11534336 | tf_op jit(solution)/shard_map/rsij,rsjm->rim/dot_general | solution.py:29
  55.7 0.0 reduce-scatter.4.cloned.1.call-update
  55.7 0.0 all-gather.6.cloned.1.call-start
  55.8 0.1 fusion.28
  55.9 27.2 %reduce-scatter.4.cloned.1.call-done = bf16[2,128,512]{1,2,0:T(8,128)(2,1)} async-done(((bf16[8,128,512]{1,2,0:T(8,128)(2,1)}), bf16[2,128,512]{1,2,0:T(8,128)(2,1)}) %reduce-scatter.4.cloned.1.call-update) | async-done | bytes 262160 | tf_op jit(solution)/shard_map/reduce_scatter | solution.py:30
  83.1 1.1 copy.16
  84.2 0.1 mul.56
  84.3 0.8 fusion.21
  85.2 0.0 reduce-scatter.6.cloned.1.call-start
  85.2 29.3 %all-gather.6.cloned.1.call-done = bf16[2048,512]{1,0:T(8,128)(2,1)} async-done(((bf16[256,512]{1,0:T(8,128)(2,1)}), bf16[2048,512]{1,0:T(8,128)(2,1)}) %all-gather.6.cloned.1.call-update) | async-done | bytes 2097168 | tf_op jit(solution)/shard_map/all_gather | solution.py:27
  114.5 7.1 %gather_fusion.1 = bf16[64,128,512]{2,1,0:T(8,128)(2,1)} fusion(bf16[16,128,512]{2,1,0:T(8,128)(2,1)} %bitcast.79, s32[1024]{0:T(1024)S(1)} %pad_clamp_fusion), kind=kCustom, calls=%fused_computation.1 | custom fusion | bytes 16777472 | tf_op jit(solution)/shard_map/gather | solution.py:28
  121.6 7.1 %fusion.15 = bf16[8,128,512]{1,2,0:T(8,128)(2,1)} fusion(bf16[8,8,128,512]{3,2,1,0:T(8,128)(2,1)} %bitcast.82, bf16[8,1,8,128,128]{4,3,2,1,0:T(8,128)(2,1)S(1)} %copy-done), kind=kOutput, calls=%fused_computation.13 | convolution fusion | flops 1074266112 | bytes 11534336 | tf_op jit(solution)/shard_map/rsij,rsjm->rim/dot_general | solution.py:29
  128.8 0.0 all-gather.8.cloned.1.call-start
  128.8 27.3 %reduce-scatter.6.cloned.1.call-done = bf16[2,128,512]{1,2,0:T(8,128)(2,1)} async-done(((bf16[8,128,512]{1,2,0:T(8,128)(2,1)}), bf16[2,128,512]{1,2,0:T(8,128)(2,1)}) %reduce-scatter.6.cloned.1.call-update) | async-done | bytes 262160 | tf_op jit(solution)/shard_map/reduce_scatter | solution.py:30
  156.2 1.8 convert_multiply_fusion.1
  157.9 1.2 copy.18
  159.2 0.8 fusion.22
  160.0 0.2 reduce-scatter.8.cloned.1.call-start
  160.3 29.0 %all-gather.8.cloned.1.call-done = bf16[2048,512]{1,0:T(8,128)(2,1)} async-done(((bf16[256,512]{1,0:T(8,128)(2,1)}), bf16[2048,512]{1,0:T(8,128)(2,1)}) %all-gather.8.cloned.1.call-update) | async-done | bytes 2097168 | tf_op jit(solution)/shard_map/all_gather | solution.py:27
  189.3 7.1 %gather_fusion.2 = bf16[64,128,512]{2,1,0:T(8,128)(2,1)} fusion(bf16[16,128,512]{2,1,0:T(8,128)(2,1)} %bitcast.78, s32[1024]{0:T(1024)S(1)} %pad_clamp_fusion), kind=kCustom, calls=%fused_computation.2 | custom fusion | bytes 16777472 | tf_op jit(solution)/shard_map/gather | solution.py:28
  196.4 7.1 %fusion.18 = bf16[8,128,512]{1,2,0:T(8,128)(2,1)} fusion(bf16[8,8,128,512]{3,2,1,0:T(8,128)(2,1)} %bitcast.80, bf16[8,1,8,128,128]{4,3,2,1,0:T(8,128)(2,1)S(1)} %copy-done), kind=kOutput, calls=%fused_computation.14 | convolution fusion | flops 1074266112 | bytes 11534336 | tf_op jit(solution)/shard_map/rsij,rsjm->rim/dot_general | solution.py:29
  203.6 27.4 %reduce-scatter.8.cloned.1.call-done = bf16[2,128,512]{1,2,0:T(8,128)(2,1)} async-done(((bf16[8,128,512]{1,2,0:T(8,128)(2,1)}), bf16[2,128,512]{1,2,0:T(8,128)(2,1)}) %reduce-scatter.8.cloned.1.call-update) | async-done | bytes 262160 | tf_op jit(solution)/shard_map/reduce_scatter | solution.py:30
  231.0 1.8 convert_multiply_fusion
  232.8 1.2 copy.20
  234.0 0.8 fusion.23
  (14 shorter events, 0.1 us)
Async XLA Ops:
  7.2 41.4 %copy-start = (bf16[8,1,8,128,128]{4,3,2,1,0:T(8,128)(2,1)S(1)}, bf16[8,1,8,128,128]{4,3,2,1,0:T(8,128)(2,1)}, u32[]{:S(2)}) copy-start(bf16[8,1,8,128,128]{4,3,2,1,0:T(8,128)(2,1)} %param.5) | copy-start | bytes 6291460
  7.2 34.3 %all-gather.4.cloned.1.call-start = ((), (), s32[]{:S(2)}) async-start(), calls=%async_computation.3 | async-start | bytes 2359296 | tf_op jit(solution)/shard_map/all_gather | solution.py:27
  7.9 75.2 %reduce-scatter.4.cloned.1.call-start = ((), (), s32[]{:S(2)}) async-start(), calls=%async_computation.4 | async-start | bytes 1310720 | tf_op jit(solution)/shard_map/reduce_scatter | solution.py:30
  48.6 7.2 %copy-start.3 = (s32[2,3]{1,0:T(2,128)S(1)}, s32[2,3]{1,0:T(2,128)}, u32[]{:S(2)}) copy-start(s32[2,3]{1,0:T(2,128)} %param.7) | copy-start | bytes 76
  55.7 58.8 %all-gather.6.cloned.1.call-start = ((), (), s32[]{:S(2)}) async-start(), calls=%async_computation.5 | async-start | bytes 2359296 | tf_op jit(solution)/shard_map/all_gather | solution.py:27
  85.2 71.0 %reduce-scatter.6.cloned.1.call-start = ((), (), s32[]{:S(2)}) async-start(), calls=%async_computation.6 | async-start | bytes 1310720 | tf_op jit(solution)/shard_map/reduce_scatter | solution.py:30
  121.6 37.6 %copy-start.2 = (bf16[256,512]{1,0:T(8,128)(2,1)S(1)}, bf16[256,512]{1,0:T(8,128)(2,1)}, u32[]{:S(2)}) copy-start(bf16[256,512]{1,0:T(8,128)(2,1)} %param.4) | copy-start | bytes 786436
  128.8 60.5 %all-gather.8.cloned.1.call-start = ((), (), s32[]{:S(2)}) async-start(), calls=%async_computation.7 | async-start | bytes 2359296 | tf_op jit(solution)/shard_map/all_gather | solution.py:27
  160.0 70.9 %reduce-scatter.8.cloned.1.call-start = ((), (), s32[]{:S(2)}) async-start(), calls=%async_computation.8 | async-start | bytes 1310720 | tf_op jit(solution)/shard_map/reduce_scatter | solution.py:30
  196.4 37.6 %copy-start.1 = (bf16[256,512]{1,0:T(8,128)(2,1)S(1)}, bf16[256,512]{1,0:T(8,128)(2,1)}, u32[]{:S(2)}) copy-start(bf16[256,512]{1,0:T(8,128)(2,1)} %fusion.21) | copy-start | bytes 786436
Sparse Core Ops, SparseCore 0:
  9.6 31.7 all-gather.3
  55.8 27.2 reduce-scatter.3
  85.4 29.0 all-gather.5
  128.9 27.2 reduce-scatter.5
  160.2 29.0 all-gather.7
  203.7 27.2 reduce-scatter.7
where the time goes:
time: 242 us
  waiting for transfers between devices  174 us (72%)
  local copies, waits for them, and re-layouts  25.2 us (10%)
  matrix products  21.4 us (9%)
  between operations  14.2 us (6%)
  other arithmetic  6.82 us (3%)
    all_gather x3, waiting for transfers between devices, apply_slab(): lax.all_gather(slab, 'row', axis=0, tiled=True).reshape(-1, BS, width)  91 us
    reduce_scatter x3, waiting for transfers between devices, apply_slab(): lax.psum_scatter(result.astype(jnp.bfloat16).astype(jnp.float32).astype(j...  81.9 us
    dot_general x3, matrix products, apply_slab(): jnp.einsum('rsij,rsjm->rim', blocks, picked, preferred_element_type=jnp.f...  21.4 us
    gather x3, local copies, waits for them, and re-layouts, apply_slab(): picked = gathered[local_index]  21.4 us
  transfers between devices with their start and end apart: 6, of which 6 were waited for; matrix products, arithmetic and copies ran while one was open for 0% of the time, Pallas kernels for 0%

commit v1 on v0

--- a/solution.py
+++ b/solution.py
@@ -5,6 +5,27 @@
 
 BS = 128
 STEPS = 3
+
+
+def collect(x, axis, dim):
+    size, here, rows = (lax.axis_size(axis), lax.axis_index(axis), x.shape[dim])
+    forward = [(i, (i + 1) % size) for i in range(size)]
+    behind = [(i, (i - 1) % size) for i in range(size)]
+    result = jnp.zeros((*x.shape[:dim], size * rows, *x.shape[dim + 1 :]), x.dtype)
+    result = lax.dynamic_update_slice_in_dim(result, x, here * rows, axis=dim)
+    from_left = from_right = x
+    halfway = size // 2
+    for step in range(1, halfway + 1):
+        from_left = lax.ppermute(from_left, axis, forward)
+        result = lax.dynamic_update_slice_in_dim(
+            result, from_left, (here - step) % size * rows, axis=dim
+        )
+        if step < size - halfway:
+            from_right = lax.ppermute(from_right, axis, behind)
+            result = lax.dynamic_update_slice_in_dim(
+                result, from_right, (here + step) % size * rows, axis=dim
+            )
+    return result
 
 
 def per_device(t_start, h_blocks, h_cols, t_cols):
@@ -24,7 +45,7 @@
         return shaped.reshape(rows_here * BS, width)
 
     def apply_slab(slab):
-        gathered = lax.all_gather(slab, "row", axis=0, tiled=True).reshape(-1, BS, width)
+        gathered = collect(slab, "row", 0).reshape(-1, BS, width)
         picked = gathered[local_index]
         result = jnp.einsum("rsij,rsjm->rim", blocks, picked, preferred_element_type=jnp.float32)
         summed = lax.psum_scatter(

time: 242 us -> 254 us (1.050)
  waiting for transfers between devices: 174 us -> 133 us
  starting transfers between devices: 0.42 us -> 32.7 us
  local copies, waits for them, and re-layouts: 25.2 us -> 46.3 us
    all_gather x3 -> x0, waiting for transfers between devices: 91 us -> none  [apply_slab(): lax.all_gather(slab, 'row', axis=0, tiled=True).reshape(-1, BS, width)]
    ppermute x0 -> x21, waiting for transfers between devices: none -> 55.5 us  [the longest x12 49.9 us: collect(): from_left = lax.ppermute(from_left, axis, forward)]
    ppermute x0 -> x21, starting transfers between devices: none -> 32.6 us  [the longest x9 32 us: collect(): from_right = lax.ppermute(from_right, axis, behind)]
    dynamic_update_slice x0 -> x22, local copies, waits for them, and re-layouts: none -> 16 us  [the longest x12 8.69 us: collect(): lax.dynamic_update_slice_in_dim(result, from_left, (here - step) % size *...]
    another operation x0 -> x3, local copies, waits for them, and re-layouts: none -> 4.59 us
    reduce_scatter x3, waiting for transfers between devices: 81.9 us -> 77.6 us  [apply_slab(): lax.psum_scatter(result.astype(jnp.bfloat16).astype(jnp.float32).astype(j...]
  transfers between devices with their start and end apart: 6 -> 24, of which waited for: 6 -> 16; matrix products, arithmetic and copies ran while one was open for 0% -> 6% of each run, Pallas kernels for 0% -> 0%
where the time goes in v1:
time: 254 us; the launch traced here: 253 us
  waiting for transfers between devices  133 us (52%)
  local copies, waits for them, and re-layouts  46.3 us (18%)
  starting transfers between devices  32.7 us (13%)
  matrix products  21.3 us (8%)
  between operations  13.9 us (5%)
  other arithmetic  6.1 us (2%)
    reduce_scatter x3, waiting for transfers between devices, apply_slab(): lax.psum_scatter(result.astype(jnp.bfloat16).astype(jnp.float32).astype(j...  77.6 us
    ppermute x12, waiting for transfers between devices, collect(): from_left = lax.ppermute(from_left, axis, forward)  49.9 us
    ppermute x9, starting transfers between devices, collect(): from_right = lax.ppermute(from_right, axis, behind)  32 us
    gather x3, local copies, waits for them, and re-layouts, apply_slab(): picked = gathered[local_index]  21.5 us
    dot_general x3, matrix products, apply_slab(): jnp.einsum('rsij,rsjm->rim', blocks, picked, preferred_element_type=jnp.f...  21.3 us
    dynamic_update_slice x12, local copies, waits for them, and re-layouts, collect(): lax.dynamic_update_slice_in_dim(result, from_left, (here - step) % size *...  8.69 us
    dynamic_update_slice x9, local copies, waits for them, and re-layouts, collect(): lax.dynamic_update_slice_in_dim(result, from_right, (here + step) % size...  6.54 us
    ppermute x9, waiting for transfers between devices, collect(): from_right = lax.ppermute(from_right, axis, behind)  5.58 us
  transfers between devices with their start and end apart: 24, of which 16 were waited for; matrix products, arithmetic and copies ran while one was open for 6% of the time, Pallas kernels for 0%

profile of v1, /device:TPU:0, one launch (start us, length us, event | category | flops | bytes accessed | tf_op | source)
XLA Modules:
  0.0 253.5 jit_solution(11444041501464159267)
XLA Ops:
  7.7 4.1 %collective-permute-start.1 = (bf16[256,512]{1,0:T(8,128)(2,1)}, bf16[256,512]{1,0:T(8,128)(2,1)S(1)}, u32[]{:S(2)}, u32[]{:S(2)}) collective-permute-start(bf16[256,512]{1,0:T(8,128)(2,1)} %param.4), channel_id=1, source_target_pairs={{0,7},{1,0},{2,1},{3,2},{4,3},{5,4},{6,5},{7,6},{8,15},{9,8},{10,9... | collective-permute-start | bytes 786440 | tf_op jit(solution)/shard_map/ppermute | solution.py:24
  11.8 4.4 %collective-permute-done = bf16[256,512]{1,0:T(8,128)(2,1)S(1)} collective-permute-done((bf16[256,512]{1,0:T(8,128)(2,1)}, bf16[256,512]{1,0:T(8,128)(2,1)S(1)}, u32[]{:S(2)}, u32[]{:S(2)}) %collective-permute-start) | collective-permute-done | bytes 262176 | tf_op jit(solution)/shard_map/ppermute | solution.py:19
  17.0 1.5 broadcast.134.clone.1
  19.3 3.5 %collective-permute-start.3 = (bf16[256,512]{1,0:T(8,128)(2,1)S(1)}, bf16[256,512]{1,0:T(8,128)(2,1)S(1)}, u32[]{:S(2)}, u32[]{:S(2)}) collective-permute-start(bf16[256,512]{1,0:T(8,128)(2,1)S(1)} %collective-permute-done.1), channel_id=1, source_target_pairs={{0,7},{1,0},{2,1},{3,2},{4,3},{5,4},{6,5},{7,6},{8,15},{9,8},{10,9... | collective-permute-start | bytes 786440 | tf_op jit(solution)/shard_map/ppermute | solution.py:24
  25.3 3.5 %collective-permute-done.3 = bf16[256,512]{1,0:T(8,128)(2,1)S(1)} collective-permute-done((bf16[256,512]{1,0:T(8,128)(2,1)S(1)}, bf16[256,512]{1,0:T(8,128)(2,1)S(1)}, u32[]{:S(2)}, u32[]{:S(2)}) %collective-permute-start.3) | collective-permute-done | bytes 262176 | tf_op jit(solution)/shard_map/ppermute | solution.py:24
  28.9 3.9 %collective-permute-start.5 = (bf16[256,512]{1,0:T(8,128)(2,1)S(1)}, bf16[256,512]{1,0:T(8,128)(2,1)S(1)}, u32[]{:S(2)}, u32[]{:S(2)}) collective-permute-start(bf16[256,512]{1,0:T(8,128)(2,1)S(1)} %collective-permute-done.3), channel_id=1, source_target_pairs={{0,7},{1,0},{2,1},{3,2},{4,3},{5,4},{6,5},{7,6},{8,15},{9,8},{10,9... | collective-permute-start | bytes 786440 | tf_op jit(solution)/shard_map/ppermute | solution.py:24
  34.9 2.0 collective-permute-done.5
  37.7 3.4 %collective-permute-done.6 = bf16[256,512]{1,0:T(8,128)(2,1)S(1)} collective-permute-done((bf16[256,512]{1,0:T(8,128)(2,1)S(1)}, bf16[256,512]{1,0:T(8,128)(2,1)S(1)}, u32[]{:S(2)}, u32[]{:S(2)}) %collective-permute-start.6) | collective-permute-done | bytes 262176 | tf_op jit(solution)/shard_map/ppermute | solution.py:19
  41.8 7.2 %gather_fusion = bf16[64,128,512]{2,1,0:T(8,128)(2,1)} fusion(bf16[16,128,512]{2,1,0:T(8,128)(2,1)} %bitcast, s32[1024]{0:T(1024)S(1)} %pad_clamp_fusion), kind=kCustom, calls=%fused_computation | custom fusion | bytes 16777472 | tf_op jit(solution)/shard_map/gather | solution.py:49
  49.0 7.1 %fusion.12 = bf16[8,128,512]{1,2,0:T(8,128)(2,1)} fusion(bf16[8,8,128,512]{3,2,1,0:T(8,128)(2,1)} %bitcast.75, bf16[8,1,8,128,128]{4,3,2,1,0:T(8,128)(2,1)S(1)} %copy-done), kind=kOutput, calls=%fused_computation.12 | convolution fusion | flops 1074266112 | bytes 11534336 | tf_op jit(solution)/shard_map/rsij,rsjm->rim/dot_general | solution.py:50
  56.3 27.6 %reduce-scatter.4.cloned.1.call-done = bf16[2,128,512]{1,2,0:T(8,128)(2,1)} async-done(((bf16[8,128,512]{1,2,0:T(8,128)(2,1)}), bf16[2,128,512]{1,2,0:T(8,128)(2,1)}) %reduce-scatter.4.cloned.1.call-update) | async-done | bytes 262160 | tf_op jit(solution)/shard_map/reduce_scatter | solution.py:51
  88.1 2.8 %collective-permute-start.8 = (bf16[256,512]{1,0:T(8,128)(2,1)S(1)}, bf16[256,512]{1,0:T(8,128)(2,1)S(1)}, u32[]{:S(2)}, u32[]{:S(2)}) collective-permute-start(bf16[256,512]{1,0:T(8,128)(2,1)S(1)} %get-tuple-element.3), channel_id=1, source_target_pairs={{0,7},{1,0},{2,1},{3,2},{4,3},{5,4},{6,5},{7,6},{8,15},{9,8},{10,9... | collective-permute-start | bytes 786440 | tf_op jit(solution)/shard_map/ppermute | solution.py:24
  90.9 5.0 %collective-permute-done.7 = bf16[256,512]{1,0:T(8,128)(2,1)S(1)} collective-permute-done((bf16[256,512]{1,0:T(8,128)(2,1)S(1)}, bf16[256,512]{1,0:T(8,128)(2,1)S(1)}, u32[]{:S(2)}, u32[]{:S(2)}) %collective-permute-start.7) | collective-permute-done | bytes 262176 | tf_op jit(solution)/shard_map/ppermute | solution.py:19
  95.9 3.5 %collective-permute-start.10 = (bf16[256,512]{1,0:T(8,128)(2,1)S(1)}, bf16[256,512]{1,0:T(8,128)(2,1)S(1)}, u32[]{:S(2)}, u32[]{:S(2)}) collective-permute-start(bf16[256,512]{1,0:T(8,128)(2,1)S(1)} %collective-permute-done.8), channel_id=1, source_target_pairs={{0,7},{1,0},{2,1},{3,2},{4,3},{5,4},{6,5},{7,6},{8,15},{9,8},{10,9... | collective-permute-start | bytes 786440 | tf_op jit(solution)/shard_map/ppermute | solution.py:24
  99.5 6.8 %collective-permute-done.9 = bf16[256,512]{1,0:T(8,128)(2,1)S(1)} collective-permute-done((bf16[256,512]{1,0:T(8,128)(2,1)S(1)}, bf16[256,512]{1,0:T(8,128)(2,1)S(1)}, u32[]{:S(2)}, u32[]{:S(2)}) %collective-permute-start.9) | collective-permute-done | bytes 262176 | tf_op jit(solution)/shard_map/ppermute | solution.py:19
  107.7 3.5 %collective-permute-start.12 = (bf16[256,512]{1,0:T(8,128)(2,1)S(1)}, bf16[256,512]{1,0:T(8,128)(2,1)S(1)}, u32[]{:S(2)}, u32[]{:S(2)}) collective-permute-start(bf16[256,512]{1,0:T(8,128)(2,1)S(1)} %collective-permute-done.10), channel_id=1, source_target_pairs={{0,7},{1,0},{2,1},{3,2},{4,3},{5,4},{6,5},{7,6},{8,15},{9,8},{10,9... | collective-permute-start | bytes 786440 | tf_op jit(solution)/shard_map/ppermute | solution.py:24
  112.0 3.4 %collective-permute-done.11 = bf16[256,512]{1,0:T(8,128)(2,1)S(1)} collective-permute-done((bf16[256,512]{1,0:T(8,128)(2,1)S(1)}, bf16[256,512]{1,0:T(8,128)(2,1)S(1)}, u32[]{:S(2)}, u32[]{:S(2)}) %collective-permute-start.11) | collective-permute-done | bytes 262176 | tf_op jit(solution)/shard_map/ppermute | solution.py:19
  117.5 5.4 %collective-permute-done.13 = bf16[256,512]{1,0:T(8,128)(2,1)S(1)} collective-permute-done((bf16[256,512]{1,0:T(8,128)(2,1)S(1)}, bf16[256,512]{1,0:T(8,128)(2,1)S(1)}, u32[]{:S(2)}, u32[]{:S(2)}) %collective-permute-start.13) | collective-permute-done | bytes 262176 | tf_op jit(solution)/shard_map/ppermute | solution.py:19
  123.6 7.2 %gather_fusion.1 = bf16[64,128,512]{2,1,0:T(8,128)(2,1)} fusion(bf16[16,128,512]{2,1,0:T(8,128)(2,1)} %bitcast.8, s32[1024]{0:T(1024)S(1)} %pad_clamp_fusion), kind=kCustom, calls=%fused_computation.1 | custom fusion | bytes 16777472 | tf_op jit(solution)/shard_map/gather | solution.py:49
  130.8 7.1 %fusion.15 = bf16[8,128,512]{1,2,0:T(8,128)(2,1)} fusion(bf16[8,8,128,512]{3,2,1,0:T(8,128)(2,1)} %bitcast.76, bf16[8,1,8,128,128]{4,3,2,1,0:T(8,128)(2,1)S(1)} %copy-done), kind=kOutput, calls=%fused_computation.13 | convolution fusion | flops 1074266112 | bytes 11534336 | tf_op jit(solution)/shard_map/rsij,rsjm->rim/dot_general | solution.py:50
  138.0 25.0 %reduce-scatter.6.cloned.1.call-done = bf16[2,128,512]{1,2,0:T(8,128)(2,1)} async-done(((bf16[8,128,512]{1,2,0:T(8,128)(2,1)}), bf16[2,128,512]{1,2,0:T(8,128)(2,1)}) %reduce-scatter.6.cloned.1.call-update) | async-done | bytes 262160 | tf_op jit(solution)/shard_map/reduce_scatter | solution.py:51
  167.4 3.5 %collective-permute-start.15 = (bf16[256,512]{1,0:T(8,128)(2,1)S(1)}, bf16[256,512]{1,0:T(8,128)(2,1)S(1)}, u32[]{:S(2)}, u32[]{:S(2)}) collective-permute-start(bf16[256,512]{1,0:T(8,128)(2,1)S(1)} %get-tuple-element.5), channel_id=1, source_target_pairs={{0,7},{1,0},{2,1},{3,2},{4,3},{5,4},{6,5},{7,6},{8,15},{9,8},{10,9... | collective-permute-start | bytes 786440 | tf_op jit(solution)/shard_map/ppermute | solution.py:24
  171.0 5.0 %collective-permute-done.14 = bf16[256,512]{1,0:T(8,128)(2,1)S(1)} collective-permute-done((bf16[256,512]{1,0:T(8,128)(2,1)S(1)}, bf16[256,512]{1,0:T(8,128)(2,1)S(1)}, u32[]{:S(2)}, u32[]{:S(2)}) %collective-permute-start.14) | collective-permute-done | bytes 262176 | tf_op jit(solution)/shard_map/ppermute | solution.py:19
  176.0 3.5 %collective-permute-start.17 = (bf16[256,512]{1,0:T(8,128)(2,1)S(1)}, bf16[256,512]{1,0:T(8,128)(2,1)S(1)}, u32[]{:S(2)}, u32[]{:S(2)}) collective-permute-start(bf16[256,512]{1,0:T(8,128)(2,1)S(1)} %collective-permute-done.15), channel_id=1, source_target_pairs={{0,7},{1,0},{2,1},{3,2},{4,3},{5,4},{6,5},{7,6},{8,15},{9,8},{10,9... | collective-permute-start | bytes 786440 | tf_op jit(solution)/shard_map/ppermute | solution.py:24
  179.5 6.8 %collective-permute-done.16 = bf16[256,512]{1,0:T(8,128)(2,1)S(1)} collective-permute-done((bf16[256,512]{1,0:T(8,128)(2,1)S(1)}, bf16[256,512]{1,0:T(8,128)(2,1)S(1)}, u32[]{:S(2)}, u32[]{:S(2)}) %collective-permute-start.16) | collective-permute-done | bytes 262176 | tf_op jit(solution)/shard_map/ppermute | solution.py:19
  187.8 3.5 %collective-permute-start.19 = (bf16[256,512]{1,0:T(8,128)(2,1)S(1)}, bf16[256,512]{1,0:T(8,128)(2,1)S(1)}, u32[]{:S(2)}, u32[]{:S(2)}) collective-permute-start(bf16[256,512]{1,0:T(8,128)(2,1)S(1)} %collective-permute-done.17), channel_id=1, source_target_pairs={{0,7},{1,0},{2,1},{3,2},{4,3},{5,4},{6,5},{7,6},{8,15},{9,8},{10,9... | collective-permute-start | bytes 786440 | tf_op jit(solution)/shard_map/ppermute | solution.py:24
  192.1 3.3 %collective-permute-done.18 = bf16[256,512]{1,0:T(8,128)(2,1)S(1)} collective-permute-done((bf16[256,512]{1,0:T(8,128)(2,1)S(1)}, bf16[256,512]{1,0:T(8,128)(2,1)S(1)}, u32[]{:S(2)}, u32[]{:S(2)}) %collective-permute-start.18) | collective-permute-done | bytes 262176 | tf_op jit(solution)/shard_map/ppermute | solution.py:19
  197.6 5.4 %collective-permute-done.20 = bf16[256,512]{1,0:T(8,128)(2,1)S(1)} collective-permute-done((bf16[256,512]{1,0:T(8,128)(2,1)S(1)}, bf16[256,512]{1,0:T(8,128)(2,1)S(1)}, u32[]{:S(2)}, u32[]{:S(2)}) %collective-permute-start.20) | collective-permute-done | bytes 262176 | tf_op jit(solution)/shard_map/ppermute | solution.py:19
  203.7 7.2 %gather_fusion.2 = bf16[64,128,512]{2,1,0:T(8,128)(2,1)} fusion(bf16[16,128,512]{2,1,0:T(8,128)(2,1)} %bitcast.14, s32[1024]{0:T(1024)S(1)} %pad_clamp_fusion), kind=kCustom, calls=%fused_computation.2 | custom fusion | bytes 16777472 | tf_op jit(solution)/shard_map/gather | solution.py:49
  210.9 7.1 %fusion.18 = bf16[8,128,512]{1,2,0:T(8,128)(2,1)} fusion(bf16[8,8,128,512]{3,2,1,0:T(8,128)(2,1)} %bitcast.74, bf16[8,1,8,128,128]{4,3,2,1,0:T(8,128)(2,1)S(1)} %copy-done), kind=kOutput, calls=%fused_computation.14 | convolution fusion | flops 1074266112 | bytes 11534336 | tf_op jit(solution)/shard_map/rsij,rsjm->rim/dot_general | solution.py:50
  218.0 25.1 %reduce-scatter.8.cloned.1.call-done = bf16[2,128,512]{1,2,0:T(8,128)(2,1)} async-done(((bf16[8,128,512]{1,2,0:T(8,128)(2,1)}), bf16[2,128,512]{1,2,0:T(8,128)(2,1)}) %reduce-scatter.8.cloned.1.call-update) | async-done | bytes 262160 | tf_op jit(solution)/shard_map/reduce_scatter | solution.py:51
  243.1 1.8 convert_multiply_fusion
  (78 shorter events, 29.4 us)
Async XLA Ops:
  7.2 41.8 %copy-start = (bf16[8,1,8,128,128]{4,3,2,1,0:T(8,128)(2,1)S(1)}, bf16[8,1,8,128,128]{4,3,2,1,0:T(8,128)(2,1)}, u32[]{:S(2)}) copy-start(bf16[8,1,8,128,128]{4,3,2,1,0:T(8,128)(2,1)} %param.5) | copy-start | bytes 6291460
  7.2 11.4 %copy-start.2 = (bf16[256,512]{1,0:T(8,128)(2,1)S(1)}, bf16[256,512]{1,0:T(8,128)(2,1)}, u32[]{:S(2)}) copy-start(bf16[256,512]{1,0:T(8,128)(2,1)} %param.4) | copy-start | bytes 786436
  7.2 76.6 %reduce-scatter.4.cloned.1.call-start = ((), (), s32[]{:S(2)}) async-start(), calls=%async_computation.3 | async-start | bytes 1310720 | tf_op jit(solution)/shard_map/reduce_scatter | solution.py:51
  7.2 9.0 %collective-permute-start = (bf16[256,512]{1,0:T(8,128)(2,1)}, bf16[256,512]{1,0:T(8,128)(2,1)S(1)}, u32[]{:S(2)}, u32[]{:S(2)}) collective-permute-start(bf16[256,512]{1,0:T(8,128)(2,1)} %param.4), channel_id=1, source_target_pairs={{0,1},{1,2},{2,3},{3,4},{4,5},{5,6},{6,7},{7,0},{8,9},{9,10},{10,1... | collective-permute-start | bytes 786440 | tf_op jit(solution)/shard_map/ppermute | solution.py:19
  7.7 11.5 %collective-permute-start.1 = (bf16[256,512]{1,0:T(8,128)(2,1)}, bf16[256,512]{1,0:T(8,128)(2,1)S(1)}, u32[]{:S(2)}, u32[]{:S(2)}) collective-permute-start(bf16[256,512]{1,0:T(8,128)(2,1)} %param.4), channel_id=1, source_target_pairs={{0,7},{1,0},{2,1},{3,2},{4,3},{5,4},{6,5},{7,6},{8,15},{9,8},{10,9... | collective-permute-start | bytes 786440 | tf_op jit(solution)/shard_map/ppermute | solution.py:24
  16.2 7.7 %collective-permute-start.2 = (bf16[256,512]{1,0:T(8,128)(2,1)S(1)}, bf16[256,512]{1,0:T(8,128)(2,1)S(1)}, u32[]{:S(2)}, u32[]{:S(2)}) collective-permute-start(bf16[256,512]{1,0:T(8,128)(2,1)S(1)} %collective-permute-done), channel_id=1, source_target_pairs={{0,1},{1,2},{2,3},{3,4},{4,5},{5,6},{6,7},{7,0},{8,9},{9,10},{10,1... | collective-permute-start | bytes 786440 | tf_op jit(solution)/shard_map/ppermute | solution.py:19
  19.3 9.6 %collective-permute-start.3 = (bf16[256,512]{1,0:T(8,128)(2,1)S(1)}, bf16[256,512]{1,0:T(8,128)(2,1)S(1)}, u32[]{:S(2)}, u32[]{:S(2)}) collective-permute-start(bf16[256,512]{1,0:T(8,128)(2,1)S(1)} %collective-permute-done.1), channel_id=1, source_target_pairs={{0,7},{1,0},{2,1},{3,2},{4,3},{5,4},{6,5},{7,6},{8,15},{9,8},{10,9... | collective-permute-start | bytes 786440 | tf_op jit(solution)/shard_map/ppermute | solution.py:24
  23.9 9.6 %collective-permute-start.4 = (bf16[256,512]{1,0:T(8,128)(2,1)S(1)}, bf16[256,512]{1,0:T(8,128)(2,1)S(1)}, u32[]{:S(2)}, u32[]{:S(2)}) collective-permute-start(bf16[256,512]{1,0:T(8,128)(2,1)S(1)} %collective-permute-done.2), channel_id=1, source_target_pairs={{0,1},{1,2},{2,3},{3,4},{4,5},{5,6},{6,7},{7,0},{8,9},{9,10},{10,1... | collective-permute-start | bytes 786440 | tf_op jit(solution)/shard_map/ppermute | solution.py:19
  28.9 8.1 %collective-permute-start.5 = (bf16[256,512]{1,0:T(8,128)(2,1)S(1)}, bf16[256,512]{1,0:T(8,128)(2,1)S(1)}, u32[]{:S(2)}, u32[]{:S(2)}) collective-permute-start(bf16[256,512]{1,0:T(8,128)(2,1)S(1)} %collective-permute-done.3), channel_id=1, source_target_pairs={{0,7},{1,0},{2,1},{3,2},{4,3},{5,4},{6,5},{7,6},{8,15},{9,8},{10,9... | collective-permute-start | bytes 786440 | tf_op jit(solution)/shard_map/ppermute | solution.py:24
  33.5 7.6 %collective-permute-start.6 = (bf16[256,512]{1,0:T(8,128)(2,1)S(1)}, bf16[256,512]{1,0:T(8,128)(2,1)S(1)}, u32[]{:S(2)}, u32[]{:S(2)}) collective-permute-start(bf16[256,512]{1,0:T(8,128)(2,1)S(1)} %collective-permute-done.4), channel_id=1, source_target_pairs={{0,1},{1,2},{2,3},{3,4},{4,5},{5,6},{6,7},{7,0},{8,9},{9,10},{10,1... | collective-permute-start | bytes 786440 | tf_op jit(solution)/shard_map/ppermute | solution.py:19
  49.0 7.2 %copy-start.6 = (s32[2,3]{1,0:T(2,128)S(1)}, s32[2,3]{1,0:T(2,128)}, u32[]{:S(2)}) copy-start(s32[2,3]{1,0:T(2,128)} %param.7) | copy-start | bytes 76
  56.1 106.9 %reduce-scatter.6.cloned.1.call-start = ((), (), s32[]{:S(2)}) async-start(), calls=%async_computation.4 | async-start | bytes 1310720 | tf_op jit(solution)/shard_map/reduce_scatter | solution.py:51
  87.4 0.7 copy-start.3
  87.4 8.5 %collective-permute-start.7 = (bf16[256,512]{1,0:T(8,128)(2,1)S(1)}, bf16[256,512]{1,0:T(8,128)(2,1)S(1)}, u32[]{:S(2)}, u32[]{:S(2)}) collective-permute-start(bf16[256,512]{1,0:T(8,128)(2,1)S(1)} %get-tuple-element.3), channel_id=1, source_target_pairs={{0,1},{1,2},{2,3},{3,4},{4,5},{5,6},{6,7},{7,0},{8,9},{9,10},{10,1... | collective-permute-start | bytes 786440 | tf_op jit(solution)/shard_map/ppermute | solution.py:19
  88.1 7.8 %collective-permute-start.8 = (bf16[256,512]{1,0:T(8,128)(2,1)S(1)}, bf16[256,512]{1,0:T(8,128)(2,1)S(1)}, u32[]{:S(2)}, u32[]{:S(2)}) collective-permute-start(bf16[256,512]{1,0:T(8,128)(2,1)S(1)} %get-tuple-element.3), channel_id=1, source_target_pairs={{0,7},{1,0},{2,1},{3,2},{4,3},{5,4},{6,5},{7,6},{8,15},{9,8},{10,9... | collective-permute-start | bytes 786440 | tf_op jit(solution)/shard_map/ppermute | solution.py:24
  95.9 10.3 %collective-permute-start.9 = (bf16[256,512]{1,0:T(8,128)(2,1)S(1)}, bf16[256,512]{1,0:T(8,128)(2,1)S(1)}, u32[]{:S(2)}, u32[]{:S(2)}) collective-permute-start(bf16[256,512]{1,0:T(8,128)(2,1)S(1)} %collective-permute-done.7), channel_id=1, source_target_pairs={{0,1},{1,2},{2,3},{3,4},{4,5},{5,6},{6,7},{7,0},{8,9},{9,10},{10,1... | collective-permute-start | bytes 786440 | tf_op jit(solution)/shard_map/ppermute | solution.py:19
  95.9 11.8 %collective-permute-start.10 = (bf16[256,512]{1,0:T(8,128)(2,1)S(1)}, bf16[256,512]{1,0:T(8,128)(2,1)S(1)}, u32[]{:S(2)}, u32[]{:S(2)}) collective-permute-start(bf16[256,512]{1,0:T(8,128)(2,1)S(1)} %collective-permute-done.8), channel_id=1, source_target_pairs={{0,7},{1,0},{2,1},{3,2},{4,3},{5,4},{6,5},{7,6},{8,15},{9,8},{10,9... | collective-permute-start | bytes 786440 | tf_op jit(solution)/shard_map/ppermute | solution.py:24
  106.2 9.1 %collective-permute-start.11 = (bf16[256,512]{1,0:T(8,128)(2,1)S(1)}, bf16[256,512]{1,0:T(8,128)(2,1)S(1)}, u32[]{:S(2)}, u32[]{:S(2)}) collective-permute-start(bf16[256,512]{1,0:T(8,128)(2,1)S(1)} %collective-permute-done.9), channel_id=1, source_target_pairs={{0,1},{1,2},{2,3},{3,4},{4,5},{5,6},{6,7},{7,0},{8,9},{9,10},{10,1... | collective-permute-start | bytes 786440 | tf_op jit(solution)/shard_map/ppermute | solution.py:19
  107.7 9.1 %collective-permute-start.12 = (bf16[256,512]{1,0:T(8,128)(2,1)S(1)}, bf16[256,512]{1,0:T(8,128)(2,1)S(1)}, u32[]{:S(2)}, u32[]{:S(2)}) collective-permute-start(bf16[256,512]{1,0:T(8,128)(2,1)S(1)} %collective-permute-done.10), channel_id=1, source_target_pairs={{0,7},{1,0},{2,1},{3,2},{4,3},{5,4},{6,5},{7,6},{8,15},{9,8},{10,9... | collective-permute-start | bytes 786440 | tf_op jit(solution)/shard_map/ppermute | solution.py:24
  115.3 7.6 %collective-permute-start.13 = (bf16[256,512]{1,0:T(8,128)(2,1)S(1)}, bf16[256,512]{1,0:T(8,128)(2,1)S(1)}, u32[]{:S(2)}, u32[]{:S(2)}) collective-permute-start(bf16[256,512]{1,0:T(8,128)(2,1)S(1)} %collective-permute-done.11), channel_id=1, source_target_pairs={{0,1},{1,2},{2,3},{3,4},{4,5},{5,6},{6,7},{7,0},{8,9},{9,10},{10,1... | collective-permute-start | bytes 786440 | tf_op jit(solution)/shard_map/ppermute | solution.py:19
  137.9 105.1 %reduce-scatter.8.cloned.1.call-start = ((), (), s32[]{:S(2)}) async-start(), calls=%async_computation.5 | async-start | bytes 1310720 | tf_op jit(solution)/shard_map/reduce_scatter | solution.py:51
  165.0 1.5 copy-start.1
  167.4 43.5 %copy-start.5 = (bf16[256,512]{1,0:T(8,128)(2,1)}, bf16[256,512]{1,0:T(8,128)(2,1)S(1)}, u32[]{:S(2)}) copy-start(bf16[256,512]{1,0:T(8,128)(2,1)S(1)} %get-tuple-element.5) | copy-start | bytes 786436
  167.4 8.6 %collective-permute-start.14 = (bf16[256,512]{1,0:T(8,128)(2,1)S(1)}, bf16[256,512]{1,0:T(8,128)(2,1)S(1)}, u32[]{:S(2)}, u32[]{:S(2)}) collective-permute-start(bf16[256,512]{1,0:T(8,128)(2,1)S(1)} %get-tuple-element.5), channel_id=1, source_target_pairs={{0,1},{1,2},{2,3},{3,4},{4,5},{5,6},{6,7},{7,0},{8,9},{9,10},{10,1... | collective-permute-start | bytes 786440 | tf_op jit(solution)/shard_map/ppermute | solution.py:19
  167.4 8.6 %collective-permute-start.15 = (bf16[256,512]{1,0:T(8,128)(2,1)S(1)}, bf16[256,512]{1,0:T(8,128)(2,1)S(1)}, u32[]{:S(2)}, u32[]{:S(2)}) collective-permute-start(bf16[256,512]{1,0:T(8,128)(2,1)S(1)} %get-tuple-element.5), channel_id=1, source_target_pairs={{0,7},{1,0},{2,1},{3,2},{4,3},{5,4},{6,5},{7,6},{8,15},{9,8},{10,9... | collective-permute-start | bytes 786440 | tf_op jit(solution)/shard_map/ppermute | solution.py:24
  176.0 10.4 %collective-permute-start.16 = (bf16[256,512]{1,0:T(8,128)(2,1)S(1)}, bf16[256,512]{1,0:T(8,128)(2,1)S(1)}, u32[]{:S(2)}, u32[]{:S(2)}) collective-permute-start(bf16[256,512]{1,0:T(8,128)(2,1)S(1)} %collective-permute-done.14), channel_id=1, source_target_pairs={{0,1},{1,2},{2,3},{3,4},{4,5},{5,6},{6,7},{7,0},{8,9},{9,10},{10,1... | collective-permute-start | bytes 786440 | tf_op jit(solution)/shard_map/ppermute | solution.py:19
  176.0 11.8 %collective-permute-start.17 = (bf16[256,512]{1,0:T(8,128)(2,1)S(1)}, bf16[256,512]{1,0:T(8,128)(2,1)S(1)}, u32[]{:S(2)}, u32[]{:S(2)}) collective-permute-start(bf16[256,512]{1,0:T(8,128)(2,1)S(1)} %collective-permute-done.15), channel_id=1, source_target_pairs={{0,7},{1,0},{2,1},{3,2},{4,3},{5,4},{6,5},{7,6},{8,15},{9,8},{10,9... | collective-permute-start | bytes 786440 | tf_op jit(solution)/shard_map/ppermute | solution.py:24
  186.3 9.1 %collective-permute-start.18 = (bf16[256,512]{1,0:T(8,128)(2,1)S(1)}, bf16[256,512]{1,0:T(8,128)(2,1)S(1)}, u32[]{:S(2)}, u32[]{:S(2)}) collective-permute-start(bf16[256,512]{1,0:T(8,128)(2,1)S(1)} %collective-permute-done.16), channel_id=1, source_target_pairs={{0,1},{1,2},{2,3},{3,4},{4,5},{5,6},{6,7},{7,0},{8,9},{9,10},{10,1... | collective-permute-start | bytes 786440 | tf_op jit(solution)/shard_map/ppermute | solution.py:19
  187.8 9.0 %collective-permute-start.19 = (bf16[256,512]{1,0:T(8,128)(2,1)S(1)}, bf16[256,512]{1,0:T(8,128)(2,1)S(1)}, u32[]{:S(2)}, u32[]{:S(2)}) collective-permute-start(bf16[256,512]{1,0:T(8,128)(2,1)S(1)} %collective-permute-done.17), channel_id=1, source_target_pairs={{0,7},{1,0},{2,1},{3,2},{4,3},{5,4},{6,5},{7,6},{8,15},{9,8},{10,9... | collective-permute-start | bytes 786440 | tf_op jit(solution)/shard_map/ppermute | solution.py:24
  195.4 7.6 %collective-permute-start.20 = (bf16[256,512]{1,0:T(8,128)(2,1)S(1)}, bf16[256,512]{1,0:T(8,128)(2,1)S(1)}, u32[]{:S(2)}, u32[]{:S(2)}) collective-permute-start(bf16[256,512]{1,0:T(8,128)(2,1)S(1)} %collective-permute-done.18), channel_id=1, source_target_pairs={{0,1},{1,2},{2,3},{3,4},{4,5},{5,6},{6,7},{7,0},{8,9},{9,10},{10,1... | collective-permute-start | bytes 786440 | tf_op jit(solution)/shard_map/ppermute | solution.py:19
  218.0 28.1 %copy-start.4 = (bf16[256,512]{1,0:T(8,128)(2,1)S(1)}, bf16[256,512]{1,0:T(8,128)(2,1)}, u32[]{:S(2)}) copy-start(bf16[256,512]{1,0:T(8,128)(2,1)} %copy-done.3) | copy-start | bytes 786436
Sparse Core Ops, SparseCore 0:
  56.2 27.5 reduce-scatter.3
  138.1 24.9 reduce-scatter.5
  218.1 24.8 reduce-scatter.7
